TPU v7x, 256 devices: a whole 4x4x8 slice. The times are simulated.
256 devices in a mesh: row: 16 (over y_hi, z), col: 16 (over x, y_lo, core).
Axes of the slice: x: 4, y: 4 (y_hi: 2, y_lo: 2; y = y_hi * 2 + y_lo), z: 8, core: 2. Of those that a mesh axis runs over, the one named last changes fastest.
Arguments:
- inputs: bfloat16 [2048, 6144], P('col', 'row'), may hold values from -6 to 6
- out_grad: bfloat16 [2048, 6144], P('col', 'row'), may hold values from -6 to 6
- preact: bfloat16 [2048, 24576], P('row', 'col'), may hold values from -6 to 6
- w_in: bfloat16 [6144, 24576], P('row', 'col'), may hold values from -0.078125 to 0.078125
- w_out: bfloat16 [24576, 6144], P('col', 'row'), may hold values from -0.0390625 to 0.0390625
Outputs:
- input_grad: bfloat16 [2048, 6144], P('col', 'row')
- w_in_grad: float32 [6144, 24576], P('row', 'col')
- w_out_grad: float32 [24576, 6144], P('col', 'row')
All inputs are finite; a program needn't handle non-finite values.
Results may differ from a plain program's by a relative error of at most 0.005.
Values may be sent and summed in bfloat16 or wider, within the bound.
No kernel may reach another device: no remote copies, remote signals or barrier semaphores. Data moves between devices by JAX's collectives and lax.ppermute only.
A program may use at most 128 MiB of HBM per device.

v0:
```python
import jax
import jax.numpy as jnp
from jax import lax
from jax.sharding import PartitionSpec as P


def gelu_value(z):
    inner = 0.7978845608 * (z + 0.044715 * z * z * z)
    return 0.5 * z * (1.0 + jnp.tanh(inner))


def gelu_slope(z):
    inner = 0.7978845608 * (z + 0.044715 * z * z * z)
    tangent = jnp.tanh(inner)
    return 0.5 * (1.0 + tangent) + 0.5 * z * (1.0 - tangent * tangent) * 0.7978845608 * (
        1.0 + 3.0 * 0.044715 * z * z
    )


def local(inputs, out_grad, preact, w_in, w_out):
    grad_panel, input_panel = (
        lax.all_gather(out_grad, "col", axis=0, tiled=True),
        lax.all_gather(inputs, "col", axis=0, tiled=True),
    )
    preact_panel = lax.all_gather(preact, "row", axis=0, tiled=True)
    pre_float = preact_panel.astype(jnp.float32)
    hidden_panel = gelu_value(pre_float).astype(jnp.bfloat16)
    rows = grad_panel
    hidden_rows = lax.psum_scatter(
        lax.dot_general(rows, w_out, (((1,), (1,)), ((), ())), preferred_element_type=jnp.float32),
        "row",
        scatter_dimension=0,
        tiled=True,
    )
    local_grad = (hidden_rows * gelu_slope(preact.astype(jnp.float32))).astype(jnp.bfloat16)
    preact_grad_panel = lax.all_gather(local_grad, "row", axis=0, tiled=True)
    w_out_grad = lax.dot_general(
        hidden_panel, grad_panel, (((0,), (0,)), ((), ())), preferred_element_type=jnp.float32
    )
    w_in_grad = lax.dot_general(
        input_panel, preact_grad_panel, (((0,), (0,)), ((), ())), preferred_element_type=jnp.float32
    )
    rows = preact_grad_panel
    input_grad = lax.psum_scatter(
        lax.dot_general(rows, w_in, (((1,), (1,)), ((), ())), preferred_element_type=jnp.float32),
        "col",
        scatter_dimension=0,
        tiled=True,
    )
    return (input_grad.astype(jnp.bfloat16), w_in_grad, w_out_grad)


def solution(mesh):
    in_specs = (P("col", "row"), P("col", "row"), P("row", "col"), P("row", "col"), P("col", "row"))
    out_specs = (P("col", "row"), P("row", "col"), P("col", "row"))
    return jax.shard_map(local, mesh=mesh, in_specs=in_specs, out_specs=out_specs, check_vma=False)
```

profile of v0, /device:TPU:32, one launch (start us, length us, event | category | flops | bytes accessed | tf_op | source)
XLA Modules:
  0.0 654.0 jit_solution(13495451200928123844)
XLA Ops:
  7.2 0.0 copy-start
  7.2 0.0 all-gather.5.cloned.1.call-start
  7.2 0.7 all-gather.5.cloned.1.call-update
  7.9 0.0 reduce-scatter.3.cloned.1.call-start
  8.0 40.2 %all-gather.5.cloned.1.call-done = bf16[2048,384]{1,0:T(8,128)(2,1)} async-done(((bf16[128,384]{1,0:T(8,128)(2,1)}), bf16[2048,384]{1,0:T(8,128)(2,1)}) %all-gather.5.cloned.1.call-update) | async-done | bytes 1572880 | tf_op jit(solution)/shard_map/all_gather | solution.py:22
  48.1 0.0 copy-done
  48.1 7.9 %fusion.20 = f32[2048,1536]{1,0:T(8,128)} fusion(bf16[2048,384]{1,0:T(8,128)(2,1)} %all-gather.5.cloned.1.call-done, bf16[1536,384]{1,0:T(8,128)(2,1)S(1)} %copy-done), kind=kOutput, calls=%fused_computation.32 | convolution fusion | flops 2415919104 | bytes 15335424 | tf_op jit(solution)/shard_map/dot_general | solution.py:30
  56.0 0.0 copy-start.2
  56.0 0.0 reduce-scatter.3.cloned.1.call-update
  56.0 0.0 all-gather.7.cloned.1.call-start
  56.1 251.2 %reduce-scatter.3.cloned.1.call-done = f32[128,1536]{1,0:T(8,128)} async-done(((f32[2048,1536]{1,0:T(8,128)}), f32[128,1536]{1,0:T(8,128)}) %reduce-scatter.3.cloned.1.call-update) | async-done | bytes 786448 | tf_op jit(solution)/shard_map/reduce_scatter | solution.py:29
  307.2 0.0 copy-done.2
  307.2 2.4 fusion.14
  309.7 0.0 all-gather.7.cloned.1.call-update
  309.7 0.0 all-gather.11.cloned.1.call-start
  309.7 0.5 all-gather.11.cloned.1.call-update
  310.3 0.0 all-gather.9.cloned.1.call-start
  310.3 0.5 all-gather.9.cloned.1.call-update
  310.8 0.0 copy-start.1
  310.9 0.2 reduce-scatter.5.cloned.1.call-start
  311.1 113.5 %all-gather.7.cloned.1.call-done = bf16[2048,1536]{1,0:T(8,128)(2,1)} async-done(((bf16[128,1536]{1,0:T(8,128)(2,1)}), bf16[2048,1536]{1,0:T(8,128)(2,1)}) %all-gather.7.cloned.1.call-update) | async-done | bytes 6291472 | tf_op jit(solution)/shard_map/all_gather | solution.py:36
  424.5 8.2 %fusion.21 = f32[2048,384]{1,0:T(8,128)} fusion(bf16[2048,1536]{1,0:T(8,128)(2,1)} %all-gather.7.cloned.1.call-done, bf16[384,1536]{1,0:T(8,128)(2,1)} %param.8), kind=kOutput, calls=%fused_computation.33 | convolution fusion | flops 2415919104 | bytes 10616832 | tf_op jit(solution)/shard_map/dot_general | solution.py:45
  432.7 0.0 reduce-scatter.5.cloned.1.call-update
  432.8 107.3 %all-gather.11.cloned.1.call-done = bf16[2048,1536]{1,0:T(8,128)(2,1)} async-done(((bf16[128,1536]{1,0:T(8,128)(2,1)}), bf16[2048,1536]{1,0:T(8,128)(2,1)}) %all-gather.11.cloned.1.call-update) | async-done | bytes 6291472 | tf_op jit(solution)/shard_map/all_gather | solution.py:25
  540.0 0.0 copy-done.1
  540.0 10.3 %fusion.5 = f32[1536,384]{1,0:T(8,128)} fusion(bf16[2048,384]{1,0:T(8,128)(2,1)S(1)} %copy-done.1, bf16[2048,1536]{1,0:T(8,128)(2,1)} %all-gather.11.cloned.1.call-done), kind=kOutput, calls=%fused_computation.10 | convolution fusion | flops 2447376384 | bytes 10223616 | tf_op jit(solution)/shard_map/dot_general | solution.py:37
  550.3 24.5 %all-gather.9.cloned.1.call-done = bf16[2048,384]{1,0:T(8,128)(2,1)} async-done(((bf16[128,384]{1,0:T(8,128)(2,1)}), bf16[2048,384]{1,0:T(8,128)(2,1)}) %all-gather.9.cloned.1.call-update) | async-done | bytes 1572880 | tf_op jit(solution)/shard_map/all_gather | solution.py:23
  574.8 6.0 convolution_bitcast_fusion
  580.8 2.0 copy.8
  582.7 62.8 %reduce-scatter.5.cloned.1.call-done = f32[128,384]{1,0:T(8,128)} async-done(((f32[2048,384]{1,0:T(8,128)}), f32[128,384]{1,0:T(8,128)}) %reduce-scatter.5.cloned.1.call-update) | async-done | bytes 196624 | tf_op jit(solution)/shard_map/reduce_scatter | solution.py:44
  645.6 1.6 convert_element_type.17
Async XLA Ops:
  7.2 41.0 %copy-start = (bf16[1536,384]{1,0:T(8,128)(2,1)S(1)}, bf16[1536,384]{1,0:T(8,128)(2,1)}, u32[]{:S(2)}) copy-start(bf16[1536,384]{1,0:T(8,128)(2,1)} %param.9) | copy-start | bytes 3538948
  7.2 41.0 %all-gather.5.cloned.1.call-start = ((), (), s32[]{:S(2)}) async-start(), calls=%async_computation.2 | async-start | bytes 1671168 | tf_op jit(solution)/shard_map/all_gather | solution.py:22
  7.9 299.3 %reduce-scatter.3.cloned.1.call-start = ((), (), s32[]{:S(2)}) async-start(), calls=%async_computation.3 | async-start | bytes 13369344 | tf_op jit(solution)/shard_map/reduce_scatter | solution.py:29
  56.0 251.2 %copy-start.2 = (bf16[128,1536]{1,0:T(8,128)(2,1)S(1)}, bf16[128,1536]{1,0:T(8,128)(2,1)}, u32[]{:S(2)}) copy-start(bf16[128,1536]{1,0:T(8,128)(2,1)} %param.7) | copy-start | bytes 1179652
  56.0 368.5 %all-gather.7.cloned.1.call-start = ((), (), s32[]{:S(2)}) async-start(), calls=%async_computation.4 | async-start | bytes 6684672 | tf_op jit(solution)/shard_map/all_gather | solution.py:36
  309.7 230.4 %all-gather.11.cloned.1.call-start = ((), (), s32[]{:S(2)}) async-start(), calls=%async_computation.7 | async-start | bytes 6684672 | tf_op jit(solution)/shard_map/all_gather | solution.py:25
  310.3 264.5 %all-gather.9.cloned.1.call-start = ((), (), s32[]{:S(2)}) async-start(), calls=%async_computation.6 | async-start | bytes 1671168 | tf_op jit(solution)/shard_map/all_gather | solution.py:23
  310.8 229.2 %copy-start.1 = (bf16[2048,384]{1,0:T(8,128)(2,1)S(1)}, bf16[2048,384]{1,0:T(8,128)(2,1)}, u32[]{:S(2)}) copy-start(bf16[2048,384]{1,0:T(8,128)(2,1)} %all-gather.5.cloned.1.call-done) | copy-start | bytes 4718596
  310.9 334.7 %reduce-scatter.5.cloned.1.call-start = ((), (), s32[]{:S(2)}) async-start(), calls=%async_computation.5 | async-start | bytes 3342336 | tf_op jit(solution)/shard_map/reduce_scatter | solution.py:44
Sparse Core Ops, SparseCore 0:
  9.9 38.2 all-gather.4
  56.2 251.0 reduce-scatter.2
  310.8 113.7 all-gather.6
  427.3 112.6 all-gather.10
  541.9 32.8 all-gather.8
  577.4 68.1 reduce-scatter.4
where the time goes:
time: 654 us
  waiting for transfers between devices  601 us (92%)
  matrix products  32.3 us (5%)
  between operations  14.1 us (2%)
    reduce_scatter x1, waiting for transfers between devices, local(): lax.psum_scatter(lax.dot_general(rows, w_out, (((1,), (1,)), ((), ())), p...  251 us
    all_gather x1, waiting for transfers between devices, local(): preact_grad_panel = lax.all_gather(local_grad, 'row', axis=0, tiled=True)  113 us
    all_gather x1, waiting for transfers between devices, local(): preact_panel = lax.all_gather(preact, 'row', axis=0, tiled=True)  107 us
    reduce_scatter x1, waiting for transfers between devices, local(): lax.psum_scatter(lax.dot_general(rows, w_in, (((1,), (1,)), ((), ())), pr...  62.8 us
    all_gather x1, waiting for transfers between devices, local(): lax.all_gather(out_grad, 'col', axis=0, tiled=True)  40.2 us
    all_gather x1, waiting for transfers between devices, local(): lax.all_gather(inputs, 'col', axis=0, tiled=True)  24.5 us
  transfers between devices with their start and end apart: 6, of which 6 were waited for; matrix products, arithmetic and copies ran while one was open for 4% of the time, Pallas kernels for 0%

commit v1 on v0

--- a/solution.py
+++ b/solution.py
@@ -33,7 +33,9 @@
         tiled=True,
     )
     local_grad = (hidden_rows * gelu_slope(preact.astype(jnp.float32))).astype(jnp.bfloat16)
-    preact_grad_panel = lax.all_gather(local_grad, "row", axis=0, tiled=True)
+    preact_grad_panel = jnp.concatenate(
+        lax.all_to_all(jnp.stack([local_grad] * lax.axis_size("row")), "row", 0, 0), axis=0
+    )
     w_out_grad = lax.dot_general(
         hidden_panel, grad_panel, (((0,), (0,)), ((), ())), preferred_element_type=jnp.float32
     )

time: 654 us -> 632 us (0.966)
  waiting for transfers between devices: 601 us -> 570 us
    all_to_all x0 -> x1, waiting for transfers between devices: none -> 162 us  [local(): lax.all_to_all(jnp.stack([local_grad] * lax.axis_size('row')), 'row', 0, 0)]
    all_gather x1 -> x0, waiting for transfers between devices: 113 us -> none  [local(): preact_grad_panel = lax.all_gather(local_grad, 'row', axis=0, tiled=True)]
    all_gather x1, waiting for transfers between devices: 107 us -> 27.9 us  [local(): preact_panel = lax.all_gather(preact, 'row', axis=0, tiled=True)]
  transfers between devices with their start and end apart: 6 -> 6, of which waited for: 6 -> 6; matrix products, arithmetic and copies ran while one was open for 4% -> 5% of each run, Pallas kernels for 0% -> 0%
where the time goes in v1:
time: 632 us; the launch traced here: 631 us
  waiting for transfers between devices  570 us (90%)
  matrix products  32.6 us (5%)
  between operations  13.8 us (2%)
  starting transfers between devices  6.81 us (1%)
    reduce_scatter x1, waiting for transfers between devices, local(): lax.psum_scatter(lax.dot_general(rows, w_out, (((1,), (1,)), ((), ())), p...  250 us
    all_to_all x1, waiting for transfers between devices, local(): lax.all_to_all(jnp.stack([local_grad] * lax.axis_size('row')), 'row', 0, 0)  162 us
    reduce_scatter x1, waiting for transfers between devices, local(): lax.psum_scatter(lax.dot_general(rows, w_in, (((1,), (1,)), ((), ())), pr...  62.8 us
    all_gather x1, waiting for transfers between devices, local(): lax.all_gather(out_grad, 'col', axis=0, tiled=True)  40.2 us
    all_gather x1, waiting for transfers between devices, local(): preact_panel = lax.all_gather(preact, 'row', axis=0, tiled=True)  27.9 us
    all_gather x1, waiting for transfers between devices, local(): lax.all_gather(inputs, 'col', axis=0, tiled=True)  24.4 us
  transfers between devices with their start and end apart: 6, of which 6 were waited for; matrix products, arithmetic and copies ran while one was open for 5% of the time, Pallas kernels for 0%

profile of v1, /device:TPU:32, one launch (start us, length us, event | category | flops | bytes accessed | tf_op | source)
XLA Modules:
  0.0 631.3 jit_solution(8090663042179594420)
XLA Ops:
  7.2 0.0 copy-start
  7.2 0.0 all-gather.4.cloned.1.call-start
  7.2 0.7 all-gather.4.cloned.1.call-update
  7.9 0.0 reduce-scatter.3.cloned.1.call-start
  8.0 40.2 %all-gather.4.cloned.1.call-done = bf16[2048,384]{1,0:T(8,128)(2,1)} async-done(((bf16[128,384]{1,0:T(8,128)(2,1)}), bf16[2048,384]{1,0:T(8,128)(2,1)}) %all-gather.4.cloned.1.call-update) | async-done | bytes 1572880 | tf_op jit(solution)/shard_map/all_gather | solution.py:22
  48.1 0.0 copy-done
  48.1 7.9 %fusion.20 = f32[2048,1536]{1,0:T(8,128)} fusion(bf16[2048,384]{1,0:T(8,128)(2,1)} %all-gather.4.cloned.1.call-done, bf16[1536,384]{1,0:T(8,128)(2,1)S(1)} %copy-done), kind=kOutput, calls=%fused_computation.32 | convolution fusion | flops 2415919104 | bytes 15335424 | tf_op jit(solution)/shard_map/dot_general | solution.py:30
  56.0 0.0 copy-start.2
  56.0 0.0 reduce-scatter.3.cloned.1.call-update
  56.0 0.0 all-gather.8.cloned.1.call-start
  56.1 0.7 all-gather.8.cloned.1.call-update
  56.8 250.5 %reduce-scatter.3.cloned.1.call-done = f32[128,1536]{1,0:T(8,128)} async-done(((f32[2048,1536]{1,0:T(8,128)}), f32[128,1536]{1,0:T(8,128)}) %reduce-scatter.3.cloned.1.call-update) | async-done | bytes 786448 | tf_op jit(solution)/shard_map/reduce_scatter | solution.py:29
  307.2 0.0 copy-done.2
  307.2 1.7 fusion.14
  308.9 3.3 stack.2
  312.1 6.4 %all-to-all-start = ((bf16[16,128,1536]{2,1,0:T(8,128)(2,1)}), bf16[16,128,1536]{2,1,0:T(8,128)(2,1)}, u32[]{:S(2)}, u32[]{:S(2)}) async-start(bf16[16,128,1536]{2,1,0:T(8,128)(2,1)} %stack.2), calls=%async_computation.1 | async-start | bytes 12582912 | tf_op jit(solution)/shard_map/all_to_all | solution.py:37
  318.6 0.0 all-gather.6.cloned.1.call-start
  318.6 0.5 all-gather.6.cloned.1.call-update
  319.2 0.2 reduce-scatter.5.cloned.1.call-start
  319.4 162.0 %all-to-all-done = bf16[16,128,1536]{2,1,0:T(8,128)(2,1)} async-done(((bf16[16,128,1536]{2,1,0:T(8,128)(2,1)}), bf16[16,128,1536]{2,1,0:T(8,128)(2,1)}, u32[]{:S(2)}, u32[]{:S(2)}) %all-to-all-start) | async-done | bytes 6291488 | tf_op jit(solution)/shard_map/all_to_all | solution.py:37
  481.4 0.0 copy-start.1
  481.4 8.4 %fusion.21 = f32[2048,384]{1,0:T(8,128)} fusion(bf16[2048,1536]{1,0:T(8,128)(2,1)} %bitcast, bf16[384,1536]{1,0:T(8,128)(2,1)} %param.8), kind=kOutput, calls=%fused_computation.33 | convolution fusion | flops 2415919104 | bytes 10616832 | tf_op jit(solution)/shard_map/dot_general | solution.py:47
  489.8 0.0 reduce-scatter.5.cloned.1.call-update
  489.9 27.9 %all-gather.8.cloned.1.call-done = bf16[2048,1536]{1,0:T(8,128)(2,1)} async-done(((bf16[128,1536]{1,0:T(8,128)(2,1)}), bf16[2048,1536]{1,0:T(8,128)(2,1)}) %all-gather.8.cloned.1.call-update) | async-done | bytes 6291472 | tf_op jit(solution)/shard_map/all_gather | solution.py:25
  517.8 0.0 copy-done.1
  517.8 10.3 %fusion.5 = f32[1536,384]{1,0:T(8,128)} fusion(bf16[2048,384]{1,0:T(8,128)(2,1)S(1)} %copy-done.1, bf16[2048,1536]{1,0:T(8,128)(2,1)} %all-gather.8.cloned.1.call-done), kind=kOutput, calls=%fused_computation.10 | convolution fusion | flops 2447376384 | bytes 10223616 | tf_op jit(solution)/shard_map/dot_general | solution.py:39
  528.1 24.4 %all-gather.6.cloned.1.call-done = bf16[2048,384]{1,0:T(8,128)(2,1)} async-done(((bf16[128,384]{1,0:T(8,128)(2,1)}), bf16[2048,384]{1,0:T(8,128)(2,1)}) %all-gather.6.cloned.1.call-update) | async-done | bytes 1572880 | tf_op jit(solution)/shard_map/all_gather | solution.py:23
  552.5 6.0 convolution_bitcast_fusion
  558.5 2.0 copy.8
  560.4 62.8 %reduce-scatter.5.cloned.1.call-done = f32[128,384]{1,0:T(8,128)} async-done(((f32[2048,384]{1,0:T(8,128)}), f32[128,384]{1,0:T(8,128)}) %reduce-scatter.5.cloned.1.call-update) | async-done | bytes 196624 | tf_op jit(solution)/shard_map/reduce_scatter | solution.py:46
  623.2 1.6 convert_element_type.17
Async XLA Ops:
  7.2 41.0 %copy-start = (bf16[1536,384]{1,0:T(8,128)(2,1)S(1)}, bf16[1536,384]{1,0:T(8,128)(2,1)}, u32[]{:S(2)}) copy-start(bf16[1536,384]{1,0:T(8,128)(2,1)} %param.9) | copy-start | bytes 3538948
  7.2 41.0 %all-gather.4.cloned.1.call-start = ((), (), s32[]{:S(2)}) async-start(), calls=%async_computation.3 | async-start | bytes 1671168 | tf_op jit(solution)/shard_map/all_gather | solution.py:22
  7.9 299.3 %reduce-scatter.3.cloned.1.call-start = ((), (), s32[]{:S(2)}) async-start(), calls=%async_computation.4 | async-start | bytes 13369344 | tf_op jit(solution)/shard_map/reduce_scatter | solution.py:29
  56.0 251.2 %copy-start.2 = (bf16[128,1536]{1,0:T(8,128)(2,1)S(1)}, bf16[128,1536]{1,0:T(8,128)(2,1)}, u32[]{:S(2)}) copy-start(bf16[128,1536]{1,0:T(8,128)(2,1)} %param.7) | copy-start | bytes 1179652
  56.0 461.8 %all-gather.8.cloned.1.call-start = ((), (), s32[]{:S(2)}) async-start(), calls=%async_computation.7 | async-start | bytes 6684672 | tf_op jit(solution)/shard_map/all_gather | solution.py:25
  312.1 169.3 %all-to-all-start = ((bf16[16,128,1536]{2,1,0:T(8,128)(2,1)}), bf16[16,128,1536]{2,1,0:T(8,128)(2,1)}, u32[]{:S(2)}, u32[]{:S(2)}) async-start(bf16[16,128,1536]{2,1,0:T(8,128)(2,1)} %stack.2), calls=%async_computation.1 | async-start | bytes 12582912 | tf_op jit(solution)/shard_map/all_to_all | solution.py:37
  318.6 233.9 %all-gather.6.cloned.1.call-start = ((), (), s32[]{:S(2)}) async-start(), calls=%async_computation.6 | async-start | bytes 1671168 | tf_op jit(solution)/shard_map/all_gather | solution.py:23
  319.2 304.1 %reduce-scatter.5.cloned.1.call-start = ((), (), s32[]{:S(2)}) async-start(), calls=%async_computation.5 | async-start | bytes 3342336 | tf_op jit(solution)/shard_map/reduce_scatter | solution.py:46
  481.4 36.4 %copy-start.1 = (bf16[2048,384]{1,0:T(8,128)(2,1)S(1)}, bf16[2048,384]{1,0:T(8,128)(2,1)}, u32[]{:S(2)}) copy-start(bf16[2048,384]{1,0:T(8,128)(2,1)} %all-gather.4.cloned.1.call-done) | copy-start | bytes 4718596
Sparse Core Ops, SparseCore 0:
  9.9 38.2 all-gather.3
  56.1 251.0 reduce-scatter.2
  310.2 207.6 all-gather.7
  519.7 32.7 all-gather.5
  555.0 68.1 reduce-scatter.4
